TPU v7x, 512 devices: a whole 4x4x16 slice. The times are simulated.
512 devices in a mesh: dp: 16 (over y, z_lo), factor: 32 (over z_hi, x, core).
Axes of the slice: x: 4, y: 4, z: 16 (z_hi: 4, z_lo: 4; z = z_hi * 4 + z_lo), core: 2. Of those that a mesh axis runs over, the one named last changes fastest.
Arguments:
- acts: bfloat16 [2048, 6144], P('dp', 'factor'), may hold values from -6 to 6
- grads_out: bfloat16 [2048, 12288], P('dp', 'factor'), may hold values from -6 to 6
- owners: int32 [136], replicated, may hold values from 0 to 31, as said below
Outputs:
- panel_rows: float32 [32, 6, 128, 512], P('factor', None, 'dp')
- precond_block: float32 [512, 512], P('factor')
Inputs may be any that keep to these rules, and one draw needn't show every extreme that they name: `owners`: each owner holds at most 6 tiles, and one owner holds exactly 6 in every draw.
All inputs are finite; a program needn't handle non-finite values.
Results may differ from a plain program's by a relative error of at most 0.0003.
Values may be sent and summed in bfloat16 or wider, within the bound.
A program may use at most 64 MiB of HBM per device.

v0:
```python
import jax
import jax.numpy as jnp
from jax import lax
from jax.sharding import PartitionSpec as P

D = 6144
PANEL = 512
TILE = 128


damping = 0.1


def apply_inverse_t(chol, rows_in):
    return jax.scipy.linalg.solve_triangular(chol, rows_in.T, lower=True).T


def slot_table(owners, owner_ids, capacity):
    tile_count = owners.shape[0]
    match = (owners[None, :] == owner_ids[:, None]).astype(jnp.int32)
    rank = jnp.cumsum(match, axis=1) - 1
    slot_ids = jnp.arange(capacity, dtype=jnp.int32)
    select = (match[:, None, :] == 1) & (rank[:, None, :] == slot_ids[None, :, None])
    valid = jnp.any(select, axis=2)
    tile_ids = jnp.sum(
        select.astype(jnp.int32) * jnp.arange(tile_count, dtype=jnp.int32)[None, None, :], axis=2
    )
    return (tile_ids, valid)


def column_starts(tile_ids, tiles_a):
    is_act = tile_ids < tiles_a
    return jnp.where(is_act, PANEL + tile_ids * TILE, D + PANEL + (tile_ids - tiles_a) * TILE)


def on_device(acts, grads_out, owners):
    tok = acts.shape[0]
    n_factor = lax.axis_size("factor")
    n_dp = lax.axis_size("dp")
    scale = 1.0 / (tok * n_dp)
    mine = lax.axis_index("factor")
    tile_count = owners.shape[0]
    tiles_a = (D - PANEL) // TILE
    capacity = max(2, 3 * tile_count // (2 * n_factor))
    act_all, grad_all = (
        lax.all_gather(acts, "factor", axis=1, tiled=True),
        lax.all_gather(grads_out, "factor", axis=1, tiled=True),
    )
    act_panel = act_all[:, :PANEL]
    grad_panel = grad_all[:, :PANEL]
    tile_mine, valid_mine = slot_table(owners, jnp.reshape(mine, (1,)), capacity)
    tile_ids = tile_mine[0]
    valid = valid_mine[0]
    starts = column_starts(tile_ids, tiles_a)
    features = jnp.concatenate([act_all, grad_all], axis=1)
    tile_cols = jax.vmap(lambda start: lax.dynamic_slice_in_dim(features, start, TILE, 1))(starts)
    width = PANEL // n_factor
    act_cols = lax.dynamic_slice_in_dim(act_panel, mine * width, width, 1)
    grad_cols = lax.dynamic_slice_in_dim(grad_panel, mine * width, width, 1)
    a_rows = jnp.dot(act_cols.T, act_panel, preferred_element_type=jnp.float32) * scale
    g_rows = jnp.dot(grad_cols.T, grad_panel, preferred_element_type=jnp.float32) * scale
    w_cols = jnp.dot(grad_panel.T, act_cols, preferred_element_type=jnp.float32) * scale
    a_rows, g_rows, w_cols = lax.psum((a_rows, g_rows, w_cols), "dp")
    a_block, g_block = (
        lax.all_gather(a_rows, "factor", axis=0, tiled=True),
        lax.all_gather(g_rows, "factor", axis=0, tiled=True),
    )
    eye = jnp.eye(PANEL, dtype=jnp.float32)
    chol_a = jnp.linalg.cholesky(a_block + damping * eye)
    chol_g = jnp.linalg.cholesky(g_block + damping * eye)
    is_act = tile_ids < tiles_a
    panels = jnp.where(is_act[:, None, None], act_panel[None], grad_panel[None])
    partial_sums = jnp.einsum("skr,skp->srp", tile_cols, panels, preferred_element_type=jnp.float32)
    partial_sums = partial_sums * (scale * valid.astype(jnp.float32))[:, None, None]
    summed = lax.psum_scatter(partial_sums, "dp", scatter_dimension=1, tiled=True)
    share = summed.shape[1]
    flat = summed.reshape(capacity * share, PANEL)
    solved_a = apply_inverse_t(chol_a, flat)
    solved_g = apply_inverse_t(chol_g, flat)
    row_is_act = jnp.repeat(is_act, share)
    solved = jnp.where(row_is_act[:, None], solved_a, solved_g)
    panel_rows = solved.reshape(1, capacity, share, PANEL)
    half_cols = jax.scipy.linalg.solve_triangular(chol_g, w_cols, lower=True)
    half_rows = lax.all_to_all(half_cols, "factor", split_axis=0, concat_axis=1, tiled=True)
    precond_block = apply_inverse_t(chol_a, half_rows)
    return (panel_rows, precond_block)


def solution(mesh):
    placed = (P("dp", "factor"), P("dp", "factor"), P())
    return jax.shard_map(
        on_device,
        mesh=mesh,
        in_specs=placed,
        out_specs=(P("factor", None, "dp", None), P("factor", None)),
        check_vma=False,
    )
```

profile of v0, /device:TPU:1, one launch (start us, length us, event | category | flops | bytes accessed | tf_op | source)
XLA Modules:
  0.0 733.4 jit_solution(17400845819925267108)
XLA Ops:
  8.7 84.0 %all-gather.5.cloned.1.call-done = bf16[128,6144]{0,1:T(8,128)(2,1)} async-done(((bf16[128,192]{0,1:T(8,128)(2,1)}), bf16[128,6144]{0,1:T(8,128)(2,1)}) %all-gather.5.cloned.1.call-update) | async-done | bytes 1572880 | tf_op jit(solution)/shard_map/all_gather | solution.py:46
  94.4 88.6 %all-gather.9.cloned.1.call-done = bf16[128,12288]{1,0:T(8,128)(2,1)} async-done(((bf16[128,384]{1,0:T(8,128)(2,1)}), bf16[128,12288]{1,0:T(8,128)(2,1)}) %all-gather.9.cloned.1.call-update) | async-done | bytes 3145744 | tf_op jit(solution)/shard_map/all_gather | solution.py:47
  186.5 147.1 %all-reduce.6.cloned.1.call-done = (f32[16,512]{1,0:T(8,128)}, f32[16,512]{1,0:T(8,128)}, f32[512,16]{0,1:T(8,128)}) async-done(((f32[16,512]{1,0:T(8,128)}, f32[16,512]{1,0:T(8,128)}, f32[512,16]{0,1:T(8,128)}), (f32[16,512]{1,0:T(8,128)}, f32[16,512]{1,0:T(8,128)}, f32[512,16]{0,1:T(8,128)})) %all-reduce.6.cloned.1.call-update) | async-done | bytes 98320 | tf_op jit(solution)/shard_map/psum | solution.py:63
  341.9 12.3 %while.9 = (s32[]{:T(128)}, bf16[128,18432]{1,0:T(8,128)(2,1)}, s32[6,2]{0,1:T(2,128)S(1)}, bf16[6,128,128]{2,1,0:T(8,128)(2,1)S(1)}, s32[]{:T(128)}) while((s32[]{:T(128)}, bf16[128,18432]{1,0:T(8,128)(2,1)}, s32[6,2]{0,1:T(2,128)S(1)}, bf16[6,128,128]{2,1,0:T(8,128)(2,1)S(1)}, s32[]{:T(128)}) %tuple.79), condition=%wide.while_cond.2, body=%wide.while_body.2.sunk | while | flops 2 | bytes 65641 | solution.py:56
  355.9 61.7 %all-gather.11.cloned.1.call-done = f32[512,512]{1,0:T(8,128)} async-done(((f32[16,512]{1,0:T(8,128)}), f32[512,512]{1,0:T(8,128)}) %all-gather.11.cloned.1.call-update) | async-done | bytes 1048592 | tf_op jit(solution)/shard_map/all_gather | solution.py:66
  419.9 11.7 %cholesky.358 = f32[128,128]{1,0:T(8,128)S(1)} custom-call(f32[128,128]{1,0:T(8,128)S(1)} %cholesky.439), custom_call_target="Cholesky" | custom-call | tf_op jit(solution)/shard_map/jit(cholesky)/cholesky | solution.py:70
  431.6 9.8 %custom-call.35 = f32[1,128,128]{1,2,0:T(8,128)S(1)} custom-call(f32[1,128,128]{2,1,0:T(8,128)S(1)} %get-tuple-element.87), custom_call_target="InvertDiagBlocksLowerTriangular" | custom-call | tf_op jit(solution)/shard_map/jit(cholesky)/cholesky | solution.py:70
  442.2 11.7 %cholesky.377 = f32[128,128]{1,0:T(8,128)S(1)} custom-call(f32[128,128]{1,0:T(8,128)S(1)} %cholesky.443), custom_call_target="Cholesky" | custom-call | tf_op jit(solution)/shard_map/jit(cholesky)/cholesky | solution.py:70
  454.0 10.0 %custom-call.36 = f32[1,128,128]{1,2,0:T(8,128)S(1)} custom-call(f32[1,128,128]{2,1,0:T(8,128)S(1)} %get-tuple-element.84), custom_call_target="InvertDiagBlocksLowerTriangular" | custom-call | tf_op jit(solution)/shard_map/jit(cholesky)/cholesky | solution.py:70
  464.7 11.7 %cholesky.398 = f32[128,128]{1,0:T(8,128)S(1)} custom-call(f32[128,128]{1,0:T(8,128)S(1)} %cholesky.448), custom_call_target="Cholesky" | custom-call | tf_op jit(solution)/shard_map/jit(cholesky)/cholesky | solution.py:70
  477.2 9.8 %custom-call.37 = f32[1,128,128]{1,2,0:T(8,128)S(1)} custom-call(f32[1,128,128]{2,1,0:T(8,128)S(1)} %get-tuple-element.81), custom_call_target="InvertDiagBlocksLowerTriangular" | custom-call | tf_op jit(solution)/shard_map/jit(cholesky)/cholesky | solution.py:70
  487.6 23.3 %cholesky.415 = f32[128,128]{1,0:T(8,128)S(1)} custom-call(f32[128,128]{1,0:T(8,128)S(1)} %convolution_subtract_fusion.4), custom_call_target="Cholesky" | custom-call | tf_op jit(solution)/shard_map/jit(cholesky)/cholesky | solution.py:70
  515.0 8.3 %while.11 = (s32[]{:T(128)}, f32[512,512]{1,0:T(8,128)S(1)}, s32[4,2]{0,1:T(2,128)S(1)}, f32[4,128,128]{2,1,0:T(8,128)S(1)}, s32[]{:T(128)}) while((s32[]{:T(128)}, f32[512,512]{1,0:T(8,128)S(1)}, s32[4,2]{0,1:T(2,128)S(1)}, f32[4,128,128]{2,1,0:T(8,128)S(1)}, s32[]{:T(128)}) %tuple.82), condition=%wide.while_cond.clone, body=%wide.while_body.clone.sunk | while | flops 2 | bytes 131189 | solution.py:15
  523.4 39.3 %custom-call.38 = f32[4,128,128]{1,2,0:T(8,128)S(1)} custom-call(f32[4,128,128]{2,1,0:T(8,128)S(1)} %get-tuple-element.42), custom_call_target="InvertDiagBlocksLowerTriangular" | custom-call | tf_op jit(solution)/shard_map/jit(_solve_triangular)/triangular_solve | solution.py:15
  565.2 7.5 %all-to-all-start = ((f32[32,1,256]{2,1,0:T(1,128)}), f32[32,1,256]{2,1,0:T(1,128)S(1)}, u32[]{:S(2)}, u32[]{:S(2)}) async-start(f32[32,1,256]{2,1,0:T(1,128)} %reshape.362), calls=%async_computation.1 | async-start | bytes 65536 | tf_op jit(solution)/shard_map/all_to_all | solution.py:84
  578.1 11.7 %cholesky.286 = f32[128,128]{1,0:T(8,128)S(1)} custom-call(f32[128,128]{1,0:T(8,128)S(1)} %cholesky.426), custom_call_target="Cholesky" | custom-call | tf_op jit(solution)/shard_map/jit(cholesky)/cholesky | solution.py:69
  589.9 9.8 %custom-call.31 = f32[1,128,128]{1,2,0:T(8,128)S(1)} custom-call(f32[1,128,128]{2,1,0:T(8,128)S(1)} %get-tuple-element.97), custom_call_target="InvertDiagBlocksLowerTriangular" | custom-call | tf_op jit(solution)/shard_map/jit(cholesky)/cholesky | solution.py:69
  602.3 11.7 %cholesky.305 = f32[128,128]{1,0:T(8,128)S(1)} custom-call(f32[128,128]{1,0:T(8,128)S(1)} %cholesky.430), custom_call_target="Cholesky" | custom-call | tf_op jit(solution)/shard_map/jit(cholesky)/cholesky | solution.py:69
  614.1 10.0 %custom-call.32 = f32[1,128,128]{1,2,0:T(8,128)S(1)} custom-call(f32[1,128,128]{2,1,0:T(8,128)S(1)} %get-tuple-element.94), custom_call_target="InvertDiagBlocksLowerTriangular" | custom-call | tf_op jit(solution)/shard_map/jit(cholesky)/cholesky | solution.py:69
  625.7 11.7 %cholesky.326 = f32[128,128]{1,0:T(8,128)S(1)} custom-call(f32[128,128]{1,0:T(8,128)S(1)} %cholesky.435), custom_call_target="Cholesky" | custom-call | tf_op jit(solution)/shard_map/jit(cholesky)/cholesky | solution.py:69
  638.1 9.8 %custom-call.33 = f32[1,128,128]{1,2,0:T(8,128)S(1)} custom-call(f32[1,128,128]{2,1,0:T(8,128)S(1)} %get-tuple-element.91), custom_call_target="InvertDiagBlocksLowerTriangular" | custom-call | tf_op jit(solution)/shard_map/jit(cholesky)/cholesky | solution.py:69
  649.4 11.9 %cholesky.343 = f32[128,128]{1,0:T(8,128)S(1)} custom-call(f32[128,128]{1,0:T(8,128)S(1)} %convolution_subtract_fusion.5), custom_call_target="Cholesky" | custom-call | tf_op jit(solution)/shard_map/jit(cholesky)/cholesky | solution.py:69
  665.4 7.9 %while.10 = (s32[]{:T(128)}, f32[512,512]{1,0:T(8,128)S(1)}, s32[4,2]{0,1:T(2,128)S(1)}, f32[4,128,128]{2,1,0:T(8,128)S(1)}, s32[]{:T(128)}) while((s32[]{:T(128)}, f32[512,512]{1,0:T(8,128)S(1)}, s32[4,2]{0,1:T(2,128)S(1)}, f32[4,128,128]{2,1,0:T(8,128)S(1)}, s32[]{:T(128)}) %tuple.98), condition=%wide.while_cond, body=%wide.while_body.sunk | while | flops 2 | bytes 131189 | solution.py:15
  673.4 39.3 %custom-call.34 = f32[4,128,128]{1,2,0:T(8,128)S(1)} custom-call(f32[4,128,128]{2,1,0:T(8,128)S(1)} %get-tuple-element.41), custom_call_target="InvertDiagBlocksLowerTriangular" | custom-call | tf_op jit(solution)/shard_map/jit(_solve_triangular)/triangular_solve | solution.py:15
  (173 shorter events, 80.6 us)
Async XLA Ops:
  7.2 85.5 %all-gather.5.cloned.1.call-start = ((), (), s32[]{:S(2)}) async-start(), calls=%async_computation.2 | async-start | bytes 1622016 | tf_op jit(solution)/shard_map/all_gather | solution.py:46
  7.9 175.1 %all-gather.9.cloned.1.call-start = ((), (), s32[]{:S(2)}) async-start(), calls=%async_computation.4 | async-start | bytes 3244032 | tf_op jit(solution)/shard_map/all_gather | solution.py:47
  8.6 325.0 %all-reduce.6.cloned.1.call-start = ((), (), s32[]{:S(2)}) async-start(), calls=%async_computation.7 | async-start | bytes 196608 | tf_op jit(solution)/shard_map/psum | solution.py:63
  186.4 231.2 %all-gather.11.cloned.1.call-start = ((), (), s32[]{:S(2)}) async-start(), calls=%async_computation.6 | async-start | bytes 1081344 | tf_op jit(solution)/shard_map/all_gather | solution.py:66
  333.6 239.1 %all-gather.7.cloned.1.call-start = ((), (), s32[]{:S(2)}) async-start(), calls=%async_computation.3 | async-start | bytes 1081344 | tf_op jit(solution)/shard_map/all_gather | solution.py:65
  337.5 378.8 %reduce-scatter.2.cloned.1.call-start = ((), (), s32[]{:S(2)}) async-start(), calls=%async_computation.5 | async-start | bytes 1671168 | tf_op jit(solution)/shard_map/reduce_scatter | solution.py:75
  441.9 120.8 %copy-start.1 = (f32[512,16]{0,1:T(8,128)S(1)}, f32[512,16]{0,1:T(8,128)}, u32[]{:S(2)}) copy-start(f32[512,16]{0,1:T(8,128)} %get-tuple-element.71) | copy-start | bytes 98308
  565.2 147.5 %all-to-all-start = ((f32[32,1,256]{2,1,0:T(1,128)}), f32[32,1,256]{2,1,0:T(1,128)S(1)}, u32[]{:S(2)}, u32[]{:S(2)}) async-start(f32[32,1,256]{2,1,0:T(1,128)} %reshape.362), calls=%async_computation.1 | async-start | bytes 65536 | tf_op jit(solution)/shard_map/all_to_all | solution.py:84
  577.1 1.0 copy-start
Sparse Core Ops, SparseCore 0:
  11.1 81.5 all-gather.4
  95.7 87.1 all-gather.8
  186.7 146.8 all-reduce.5
  337.1 80.4 all-gather.10
  421.1 66.2 all-gather.6
  490.3 77.1 reduce-scatter.1
where the time goes:
time: 744 us; the launch traced here: 733 us
  waiting for transfers between devices  383 us (51%)
  other arithmetic  258 us (35%)
  local copies, waits for them, and re-layouts  40.5 us (5%)
  matrix products  24.1 us (3%)
  between operations  20.2 us (3%)
  starting transfers between devices  7.69 us (1%)
    psum x1, waiting for transfers between devices, on_device(): a_rows, g_rows, w_cols = lax.psum((a_rows, g_rows, w_cols), 'dp')  147 us
    another operation x14, other arithmetic, on_device(): chol_g = jnp.linalg.cholesky(g_block + damping * eye)  90.3 us
    all_gather x1, waiting for transfers between devices, on_device(): lax.all_gather(grads_out, 'factor', axis=1, tiled=True)  88.6 us
    all_gather x1, waiting for transfers between devices, on_device(): lax.all_gather(acts, 'factor', axis=1, tiled=True)  84 us
    another operation x14, other arithmetic, on_device(): chol_a = jnp.linalg.cholesky(a_block + damping * eye)  78.9 us
    another operation x5, other arithmetic, apply_inverse_t(): return jax.scipy.linalg.solve_triangular(chol, rows_in.T, lower=True).T  78.9 us
    all_gather x1, waiting for transfers between devices, on_device(): lax.all_gather(g_rows, 'factor', axis=0, tiled=True)  61.7 us
    another operation x27, local copies, waits for them, and re-layouts, apply_inverse_t(): return jax.scipy.linalg.solve_triangular(chol, rows_in.T, lower=True).T  16.1 us
  transfers between devices with their start and end apart: 7, of which 4 were waited for; matrix products, arithmetic and copies ran while one was open for 42% of the time, Pallas kernels for 0%

commit v1 on v0

v1 whole, which is shorter than its diff:
```python
import jax
import jax.numpy as jnp
from jax import lax
from jax.experimental import pallas as pl
from jax.experimental.pallas import tpu as pltpu
from jax.sharding import PartitionSpec as P

D = 6144
PANEL = 512
TILE = 128
NT = 136
TILES_A = (D - PANEL) // TILE
CAP = 6
BLK = 128
GROUPS = 5
FROWS = 48

damping = 0.1
MESH = pl.DeviceIdType.MESH
HIGH = lax.Precision.HIGHEST


def lanes(x, c):
    return jnp.broadcast_to(x[:, :, c:c + 1], x.shape)


def rows8(x, j):
    return jnp.broadcast_to(x[:, j:j + 1, :], x.shape)


def strip16(x0, x1, w0, w1, c0, sub):
    b0 = [lanes(x0, c0 + j) for j in range(16)]
    b1 = [lanes(x1, c0 + j) for j in range(16)]
    d0 = jnp.ones(x0.shape, jnp.float32)
    d1 = d0
    for j in range(8):
        piv = rows8(b0[j], j)
        d0 = jnp.where(sub == j, piv, d0)
        inv = 1.0 / piv
        m0 = jnp.where(sub > j, b0[j] * inv, 0.0)
        m1 = b1[j] * inv
        for k in range(j + 1, 16):
            r = rows8(b0[k], j)
            b0[k] = b0[k] - m0 * r
            b1[k] = b1[k] - m1 * r
        r = rows8(x0, j)
        x0 = x0 - m0 * r
        x1 = x1 - m1 * r
        r = rows8(w0, j)
        w0 = w0 - m0 * r
        w1 = w1 - m1 * r
    for j in range(8):
        piv = rows8(b1[8 + j], j)
        d1 = jnp.where(sub == j, piv, d1)
        if j == 7:
            break
        m1 = jnp.where(sub > j, b1[8 + j] * (1.0 / piv), 0.0)
        for k in range(j + 1, 8):
            b1[8 + k] = b1[8 + k] - m1 * rows8(b1[8 + k], j)
        x1 = x1 - m1 * rows8(x1, j)
        w1 = w1 - m1 * rows8(w1, j)
    s0, s1 = lax.rsqrt(d0), lax.rsqrt(d1)
    s0 = s0 * (1.5 - 0.5 * d0 * s0 * s0)
    s1 = s1 * (1.5 - 0.5 * d1 * s1 * s1)
    return x0 * s0, x1 * s1, w0 * s0, w1 * s1


def factor_blocks(x, out):
    sub = lax.broadcasted_iota(jnp.int32, (2, 8, BLK), 1)
    w = jnp.where(lax.broadcasted_iota(jnp.int32, (2, BLK, BLK), 1)
                  == lax.broadcasted_iota(jnp.int32, (2, BLK, BLK), 2), 1.0, 0.0).astype(jnp.float32)
    for i in range(8):
        v0, v1, u0, u1 = strip16(x[:, 0:8], x[:, 8:16], w[:, 0:8], w[:, 8:16], 16 * i, sub)
        out[:, 16 * i:16 * i + 8, :] = u0
        out[:, 16 * i + 8:16 * i + 16, :] = u1
        if i == 7:
            break
        x, w = x[:, 16:], w[:, 16:]
        lo = 16 * (i + 1)
        for v, u in ((v0, u0), (v1, u1)):
            vt = jnp.stack([v[0].T, v[1].T])[:, lo:, :]
            for j in range(8):
                m = jnp.broadcast_to(vt[:, :, j:j + 1], x.shape)
                x = x - m * v[:, j:j + 1, :]
                w = w - m * u[:, j:j + 1, :]


def dot32(a, b, dims):
    return lax.dot_general(a, b, (dims, ((), ())), precision=HIGH, preferred_element_type=jnp.float32)


def dot16(a, b, dims):
    return lax.dot_general(a, b, (dims, ((), ())), preferred_element_type=jnp.float32)


def owned_table(own_ref, d, f):
    def look(t, carry):
        n, slots = carry[0], carry[1:]
        hit = own_ref[t] == f
        slots = tuple(
            jnp.where(jnp.logical_and(hit, n == s), t, slots[s]) for s in range(CAP))
        return (n + hit.astype(jnp.int32),) + slots

    zero = jnp.int32(0)
    found = lax.fori_loop(0, NT, look, (zero,) + (zero,) * CAP)
    n, p = found[0], lax.div(d, 8)
    table = []
    for s in range(CAP):
        t = found[1 + s]
        half = 2 * (t + 4) + p
        fa = lax.div(half, 3)
        slot_a = lax.div(half - 3 * fa - lax.rem(3 * fa + p, 2), 2)
        tg = jnp.maximum(t - TILES_A, 0) + 4
        fg = lax.div(tg, 3)
        slot_g = 2 + tg - 3 * fg
        is_act = (t < TILES_A).astype(jnp.int32)
        place = jnp.where(is_act == 1, fa * GROUPS + slot_a, fg * GROUPS + slot_g)
        table.append((place, is_act, (s < n).astype(jnp.int32)))
    return table


def kernel(own_ref, za, gr, fs, rows_out, pre_out,
           pan, feat, z0, z1, mat, inv, inv0, wmat, raw, allr, picked,
           s_one, r_one, s_z, r_blk, s_y, s_half, r_half, s_sib, r_sib, s_f, r_f,
           s_gz, s_gx, s_gs, r_g):
    d = lax.axis_index("dp")
    f = lax.axis_index("factor")
    y, zl = lax.div(d, 4), lax.rem(d, 4)
    role, zh, core = lax.rem(f, 8), lax.div(f, 8), lax.rem(f, 2)
    xx = lax.div(role, 2)
    base = f - role
    sib = f + 1 - 2 * core
    scale = 1.0 / 2048.0

    def z_peer(k):
        return lax.rem(f + 8 * k, 32)

    def x_peer(k):
        return base + 2 * lax.rem(xx + k, 4) + core

    def copy(src, dst, send, recv, to):
        return pltpu.make_async_remote_copy(
            src_ref=src, dst_ref=dst, send_sem=send, recv_sem=recv,
            device_id=to, device_id_type=MESH)

    barrier = pltpu.get_barrier_semaphore()
    for k in range(1, 16):
        pl.semaphore_signal(barrier, inc=1, device_id=(lax.rem(d + k, 16), f), device_id_type=MESH)
    for k in range(1, 4):
        pl.semaphore_signal(barrier, inc=1, device_id=(d, z_peer(k)), device_id_type=MESH)
        pl.semaphore_signal(barrier, inc=1, device_id=(d, x_peer(k)), device_id_type=MESH)
    pl.semaphore_signal(barrier, inc=1, device_id=(d, sib), device_id_type=MESH)
    pl.semaphore_wait(barrier, 22)

    places = [
        (0, z0),
        (0, pan.at[1, d, :, pl.ds(0, 384)]),
        (1, z1),
        (1, pan.at[1, d, :, pl.ds(384, 128)]),
        (2, pan.at[0, d, :, pl.ds(384, 128)]),
    ]
    held = [[n for n in range(5) if places[n][0] == r] for r in range(3)]

    def piece(n, slot, to):
        return copy(places[n][1], places[n][1], s_one.at[n, slot], r_one.at[n], (d, to))

    @pl.when(f == 0)
    def _():
        z0[...] = za[...]
        pan[1, d, :, 0:384] = gr[...]

    @pl.when(f == 1)
    def _():
        z1[...] = za[...]
        pan[1, d, :, 384:512] = gr[:, 0:128]

    @pl.when(f == 2)
    def _():
        pan[0, d, :, 384:512] = za[:, 0:128]

    for r in range(3):
        @pl.when(f == r)
        def _():
            for k in (1, 3, 2):
                for n in held[r]:
                    piece(n, k - 1, z_peer(k)).start()

        @pl.when(jnp.logical_and(role == r, zh > 0))
        def _():
            for n in held[r]:
                piece(n, 0, sib).wait_recv()

        @pl.when(role == r)
        def _():
            for k in (1, 3, 2):
                for n in held[r]:
                    piece(n, 2 + k, x_peer(k)).start()
            for n in held[r]:
                piece(n, 6, sib).start()

    def features(k):
        to = lax.rem(d + k, 16)
        return copy(fs.at[to], feat.at[d], s_f.at[k], r_f.at[k], (to, f))

    for k in range(1, 16):
        features(k).start()
    feat[d] = fs[d]
    mat[...] = jnp.zeros_like(mat)
    wmat[...] = jnp.zeros_like(wmat)
    raw[...] = jnp.zeros_like(raw)
    inv[...] = jnp.zeros_like(inv)

    for r in range(3):
        @pl.when(jnp.logical_and(core == r % 2, role != r))
        def _():
            for n in held[r]:
                piece(n, 0, sib).wait_recv()
                piece(n, 6, sib).start()
    for r in range(3):
        @pl.when(core != r % 2)
        def _():
            for n in held[r]:
                piece(n, 0, sib).wait_recv()

    pan[0, d, :, 0:128] = z0[:, 0:128]
    pan[0, d, :, 128:256] = z0[:, 128:256] + z1[:, 0:128]
    pan[0, d, :, 256:384] = z1[:, 128:256]

    def at(dy, dz):
        return lax.rem(y + 4 - dy, 4) * 4 + lax.rem(zl + 4 - dz, 4)

    def y_dev(dy):
        return (lax.rem(y + dy, 4) * 4 + zl, f)

    def block(which, sem, to):
        return copy(pan.at[core, which], pan.at[core, which], sem, r_blk.at[which], to)

    def z_copy(dz):
        return block(d, s_z.at[dz], (y * 4 + lax.rem(zl + dz, 4), f))

    def y_copy(dz, way):
        return block(at(0, dz), s_y.at[dz, way], y_dev((1, 3)[way]))

    def half_copy(dz, way):
        which = at((1, 3)[way], dz)
        ref = pan.at[core, which, pl.ds(64 * way, 64)]
        return copy(ref, ref, s_half.at[dz, way], r_half.at[way, which], y_dev((1, 3)[way]))

    def half_in(dz, way):
        which = at(2, dz)
        ref = pan.at[core, which, pl.ds(64 * way, 64)]
        return copy(ref, ref, s_half.at[dz, way], r_half.at[way, which], y_dev(1))

    def sibling(dy, dz):
        which = at(dy, dz)
        return copy(pan.at[core, which], pan.at[core, which], s_sib.at[dy * 4 + dz], r_sib.at[which], (d, sib))

    def from_sibling(dy, dz):
        which = at(dy, dz)
        return copy(pan.at[1 - core, which], pan.at[1 - core, which], s_sib.at[1], r_sib.at[which], (d, sib))

    order = (0, 1, 3, 2)
    for dz in (1, 3, 2):
        z_copy(dz).start()
    for way in range(2):
        y_copy(0, way).start()
    for dz in (1, 3, 2):
        block(at(0, dz), s_z.at[dz], y_dev(1)).wait_recv()
        for way in range(2):
            y_copy(dz, way).start()
        sibling(0, dz).start()

    def line(dy):
        return pl.ds(pl.multiple_of(lax.rem(y + 4 - dy, 4) * 4, 4), 4)

    def ready(dy):
        for dz in range(4):
            if dy or dz:
                from_sibling(dy, dz).wait_recv()

    def sum_a(dy):
        pa = pan[0, line(dy)].reshape(512, PANEL)
        mat[0] = mat[0] + dot16(pa, pa, ((0,), (0,)))

    def sum_g(dy):
        pg = pan[1, line(dy)].reshape(512, PANEL)
        mat[1] = mat[1] + dot16(pg, pg, ((0,), (0,)))

    def sum_w(dy):
        pa = pan[0, line(dy)].reshape(512, PANEL)
        pg = pan[1, line(dy)].reshape(512, PANEL)
        wmat[...] = wmat[...] + dot16(pg, pa, ((0,), (0,)))

    def sum_rows(dy):
        ra = jnp.zeros((16, PANEL), jnp.float32)
        rg = jnp.zeros((32, PANEL), jnp.float32)
        for dz in range(4):
            which = at(dy, dz)
            ra = ra + dot16(feat[which, 0:16, :], pan[0, which], ((1,), (0,)))
            rg = rg + dot16(feat[which, 16:48, :], pan[1, which], ((1,), (0,)))
        raw[0:16, :] = raw[0:16, :] + ra
        raw[16:48, :] = raw[16:48, :] + rg

    work = (sum_a, sum_g, sum_w, sum_rows)
    ready(0)
    for k in range(1, 16):
        src = lax.rem(d + 16 - k, 16)
        copy(fs.at[d], feat.at[src], s_f.at[k], r_f.at[k], (lax.rem(d + 1, 16), f)).wait_recv()
    for step in range(4):
        dz = order[step]
        for way in range(2):
            block(at((1, 3)[way], dz), s_z.at[1], y_dev(1)).wait_recv()
            half_copy(dz, way).start()
            sibling((1, 3)[way], dz).start()
        work[step](0)
    ready(1)
    for step in range(4):
        dz = order[step]
        for way in range(2):
            half_in(dz, way).wait_recv()
        sibling(2, dz).start()
        work[step](1)
    ready(3)
    for fn in work:
        fn(3)
    ready(2)
    sum_rows(2)

    for s in range(GROUPS):
        allr[f, s] = raw[8 * s:8 * s + 8, :] * scale

    def g_z(k):
        return copy(allr.at[f], allr.at[f], s_gz.at[k], r_g.at[f], (d, z_peer(k)))

    def g_x(q, k):
        src = lax.rem(f + 8 * q, 32)
        return copy(allr.at[src], allr.at[src], s_gx.at[q, k], r_g.at[src], (d, x_peer(k)))

    def g_from(q, k):
        return lax.rem(zh + q, 4) * 8 + 2 * lax.rem(xx + k, 4) + core

    def g_sib(q, k):
        src = g_from(q, k)
        return copy(allr.at[src], allr.at[src], s_gs.at[q, k], r_g.at[src], (d, sib))

    def g_in(src):
        return copy(allr.at[src], allr.at[src], s_gz.at[0], r_g.at[src], (d, sib))

    for k in (1, 3, 2):
        g_z(k).start()
        g_x(0, k).start()
    g_sib(0, 0).start()

    sum_a(2)
    sum_g(2)
    sum_w(2)

    r_i = lax.broadcasted_iota(jnp.int32, (PANEL, PANEL), 0)
    c_i = lax.broadcasted_iota(jnp.int32, (PANEL, PANEL), 1)
    shift = jnp.where(r_i == c_i, jnp.float32(damping), jnp.float32(0.0))
    mat[0] = mat[0] * scale + shift
    mat[1] = mat[1] * scale + shift

    def step(k, carry):
        start = pl.multiple_of(k * BLK, BLK)
        factor_blocks(mat[:, pl.ds(start, BLK), pl.ds(start, BLK)], inv0)
        for kk in range(4):
            @pl.when(k == kk)
            def _():
                lo, hi = kk * BLK, (kk + 1) * BLK
                for n in range(2):
                    li = inv0[n]
                    inv[n, lo:hi, lo:hi] = li
                    if kk > 0:
                        inv[n, lo:hi, 0:lo] = dot32(li, inv[n, lo:hi, 0:lo], ((1,), (0,)))
                    if kk < 3:
                        u = dot32(li, mat[n, lo:hi, hi:PANEL], ((1,), (0,)))
                        mat[n, hi:PANEL, hi:PANEL] = mat[n, hi:PANEL, hi:PANEL] - dot32(u, u, ((0,), (0,)))
                        inv[n, hi:PANEL, 0:hi] = inv[n, hi:PANEL, 0:hi] - dot32(
                            u, inv[n, lo:hi, 0:hi], ((0,), (0,)))
                if kk == 1:
                    for q in (1, 3, 2):
                        g_in(g_from(q, 0)).wait_recv()
                        for k2 in (1, 3, 2):
                            g_x(q, k2).start()
                        g_sib(q, 0).start()
        return carry

    lax.fori_loop(0, 4, step, 0)
    for q in range(4):
        for k in (1, 3, 2):
            g_in(g_from(q, k)).wait_recv()
            g_sib(q, k).start()

    mine = pl.multiple_of(f * 16, 16)
    half = dot32(inv[1, pl.ds(mine, 16), :], wmat[...] * scale, ((1,), (0,)))
    pre_out[...] = dot32(half, inv[0], ((1,), (1,)))

    table = owned_table(own_ref, d, f)
    for q in range(4):
        for k in range(4):
            g_in(g_from(q, k) + 1 - 2 * core).wait_recv()
    for s in range(CAP):
        picked[8 * s:8 * s + 8, :] = allr[lax.div(table[s][0], GROUPS), lax.rem(table[s][0], GROUPS)]
    rows = picked[...]
    ra, rg = dot32(rows, inv[0], ((1,), (1,))), dot32(rows, inv[1], ((1,), (1,)))
    for s in range(CAP):
        lo, hi = 8 * s, 8 * s + 8
        out = jnp.where(jnp.full((8, PANEL), table[s][1]) == 1, ra[lo:hi, :], rg[lo:hi, :])
        rows_out[s] = jnp.where(jnp.full((8, PANEL), table[s][2]) == 1, out, 0.0)

    for r in range(3):
        @pl.when(f == r)
        def _():
            for k in (1, 2, 3):
                for n in held[r]:
                    piece(n, k - 1, z_peer(k)).wait_send()

        @pl.when(role == r)
        def _():
            for k in (1, 2, 3):
                for n in held[r]:
                    piece(n, 2 + k, x_peer(k)).wait_send()

        @pl.when(core == r % 2)
        def _():
            for n in held[r]:
                piece(n, 6, sib).wait_send()

    for k in range(1, 16):
        features(k).wait_send()
        sibling(k // 4, k % 4).wait_send()
    for k in (1, 2, 3):
        z_copy(k).wait_send()
        g_z(k).wait_send()
    for dz in range(4):
        for way in range(2):
            y_copy(dz, way).wait_send()
            half_copy(dz, way).wait_send()
        for k in (1, 2, 3):
            g_x(dz, k).wait_send()
        for k in range(4):
            g_sib(dz, k).wait_send()


def window(owners, za, gr, fs):
    vmem = pl.BlockSpec(memory_space=pltpu.VMEM)
    dma = pltpu.SemaphoreType.DMA
    f32, bf16 = jnp.float32, jnp.bfloat16
    return pl.pallas_call(
        kernel,
        out_shape=(
            jax.ShapeDtypeStruct((CAP, 8, PANEL), f32),
            jax.ShapeDtypeStruct((16, PANEL), f32),
        ),
        in_specs=[pl.BlockSpec(memory_space=pltpu.SMEM)] + [vmem] * 3,
        out_specs=(vmem, vmem),
        scratch_shapes=[
            pltpu.VMEM((2, 16, 128, PANEL), bf16),
            pltpu.VMEM((16, FROWS, 128), bf16),
            pltpu.VMEM((128, 256), bf16),
            pltpu.VMEM((128, 256), bf16),
            pltpu.VMEM((2, PANEL, PANEL), f32),
            pltpu.VMEM((2, PANEL, PANEL), f32),
            pltpu.VMEM((2, BLK, BLK), f32),
            pltpu.VMEM((PANEL, PANEL), f32),
            pltpu.VMEM((FROWS, PANEL), f32),
            pltpu.VMEM((32, GROUPS, 8, PANEL), f32),
            pltpu.VMEM((8 * CAP, PANEL), f32),
            dma((5, 7)), dma((5,)),
            dma((4,)), dma((16,)), dma((4, 2)),
            dma((4, 2)), dma((2, 16)),
            dma((16,)), dma((16,)),
            dma((16,)), dma((16,)),
            dma((4,)), dma((4, 4)), dma((4, 4)), dma((32,)),
        ],
        compiler_params=pltpu.CompilerParams(
            collective_id=0, has_side_effects=True, vmem_limit_bytes=48 * 2**20),
        name="window",
    )(owners, za, gr, fs)


def feature_slots(acts, grads_out, odd):
    x = acts.T.reshape(3, 8, 8, 128)
    both = jnp.stack([x[0], x[2]])
    one = jnp.stack([x[1], x[1]])
    first = jnp.where(odd, one, both)
    second = jnp.where(odd, both, one)
    a = jnp.stack([first, second]).transpose(0, 2, 1, 3, 4).reshape(16, 16, 128)
    g = grads_out.T.reshape(3, 16, 8, 128).transpose(1, 0, 2, 3).reshape(16, 24, 128)
    return jnp.concatenate([a, g, jnp.zeros((16, 8, 128), a.dtype)], axis=1)


def on_device(acts, grads_out, owners):
    odd = lax.rem(lax.axis_index("factor"), 2) == 1
    zero = jnp.zeros((128, 64), acts.dtype)
    za = jnp.where(odd, jnp.concatenate([zero, acts], 1), jnp.concatenate([acts, zero], 1))
    rows, pre = window(owners, za, grads_out, feature_slots(acts, grads_out, odd))
    return rows[None], pre


def solution(mesh):
    return jax.shard_map(
        on_device,
        mesh=mesh,
        in_specs=(P("dp", "factor"), P("dp", "factor"), P()),
        out_specs=(P("factor", None, "dp", None), P("factor", None)),
        check_vma=False,
    )
```

time: 744 us -> 120 us (0.16)
  the two profiles are of different devices: /device:TPU:1 before, /device:TPU:69 now
where the time goes in v1:
time: 120 us; the launch traced here: 119 us
  Pallas kernels  114 us (95%)
  local copies, waits for them, and re-layouts  4.46 us (4%)
    pallas_call x1, Pallas kernels, window(): pl.pallas_call(kernel, out_shape=(jax.ShapeDtypeStruct((CAP, 8, PANEL), f...  114 us
    unnamed x10, local copies, waits for them, and re-layouts  3.6 us

profile of v1, /device:TPU:69, one launch (start us, length us, event | category | flops | bytes accessed | tf_op | source)
XLA Modules:
  0.0 119.5 jit_solution(3662090465146974717)
XLA Ops:
  0.6 0.8 slice_bitcast_fusion.1
  1.4 0.0 copy-start
  1.4 0.9 copy-done
  2.3 0.1 copy.18
  2.4 0.1 pad.4.clone
  2.5 0.0 copy-start.2
  2.5 0.1 maximum_maximum_fusion.fs
  2.6 0.7 copy-done.2
  3.3 0.1 copy.12
  3.4 0.0 copy-start.1
  3.4 0.1 pad_select_fusion.za
  3.5 0.6 copy-done.1
  4.1 114.1 %window.1 = (f32[6,8,512]{2,1,0:T(8,128)S(1)}, f32[16,512]{1,0:T(8,128)S(1)}) custom-call(s32[136]{0:T(256)S(1)} %copy-done.1, bf16[128,256]{1,0:T(8,128)(2,1)S(1)} %pad_select_fusion.za, bf16[128,384]{1,0:T(8,128)(2,1)S(1)} %copy-done, bf16[16,48,128]{2,1,0:T(8,128)(2,1)S(1)} %maximum_maximum_fusion.fs), custom_call_target="tpu_custom_call" | custom-call | tf_op jit(solution)/shard_map/window/pallas_call | solution.py:450
  118.2 0.6 copy.24
  118.9 0.6 copy.25
  (4 shorter events, 0.0 us)
Async XLA Ops:
  1.4 0.9 copy-start
  2.5 0.8 copy-start.2
  3.4 0.7 copy-start.1
